TPU v7x, 256 devices: a whole 4x4x8 slice. The times are simulated.
256 devices in a mesh: dp: 64 (over z, y, core), grp: 4 (over x).
Axes of the slice: x: 4, y: 4, z: 8, core: 2. Of those that a mesh axis runs over, the one named last changes fastest.
Arguments:
- grads: bfloat16 [64, 8, 2048, 128], P('dp', 'grp'), parts along dimension 1, may hold values from -6 to 6
- residual: float32 [64, 8, 2048, 128], P('dp', 'grp'), parts along dimension 1, may hold values from -4 to 4
- params: float32 [8, 2048, 128], P('grp'), parts along dimension 0, may hold values from -6 to 6
- momentum: float32 [8, 64, 63, 128], P('grp', 'dp'), parts along dimension 0, may hold values from -6 to 6
- indices: int32 [64, 8, 16], P('dp', 'grp'), parts along dimension 1, may hold values from 0 to 2047, as said below
- counts: int32 [64, 8], P('dp', 'grp'), parts along dimension 1, may hold values from 1 to 16
- region_sizes: int32 [8, 64], P('grp'), parts along dimension 0, may hold values from 1 to 63, as said below
Outputs:
- new_residual: float32 [64, 8, 2048, 128], P('dp', 'grp'), parts along dimension 1
- new_momentum: float32 [8, 64, 63, 128], P('grp', 'dp'), parts along dimension 0
- new_params: float32 [8, 2048, 128], P('grp'), parts along dimension 0
There are 4 independent parts, one for each index of `grp`. A program takes and returns all parts, laid end to end along the dimension named above; each array names one. Nothing has to cross between parts.
Inputs may be any that keep to these rules, and one draw needn't show every extreme that they name: `indices`: the 16 entries of one replica's list for one bucket are distinct. `region_sizes`: a bucket's sizes sum to 2048.
All inputs are finite; a program needn't handle non-finite values.
Results may differ from a plain program's by a relative error of at most 0.0003.
Values sent between devices are 32-bit elements; how exact they have to be, the bound alone decides.
A program may use at most 64 MiB of HBM per device.

v0:
```python
import jax
import jax.numpy as jnp
from jax import lax
from jax.sharding import PartitionSpec as P

decay_rate = 0.9
learn_rate = 0.1


def on_device(grads, residual, params, momentum, indices, counts, region_sizes):
    nblocks = grads.shape[2]
    block_width = grads.shape[3]
    listed = indices.shape[2]
    rows_max = momentum.shape[2]
    my_index = lax.axis_index("dp")
    accumulated = residual[0] + grads[0].astype(jnp.float32)
    selected = indices[0]
    active = jnp.arange(listed, dtype=jnp.int32)[None, :] < counts[0][:, None]
    blocks = jnp.arange(nblocks, dtype=jnp.int32)
    matches = (selected[:, :, None] == blocks[None, None, :]) & active[:, :, None]
    chosen = jnp.any(matches, axis=1)
    new_residual = jnp.where(chosen[:, :, None], jnp.float32(0.0), accumulated)
    starts = jnp.cumsum(region_sizes, axis=1) - region_sizes
    slot_ids = jnp.arange(rows_max, dtype=jnp.int32)
    tail_zeros = jnp.zeros((2, rows_max, block_width), jnp.float32)

    def window(source, first):
        return lax.dynamic_slice_in_dim(source, first, rows_max, 0)

    retained = jnp.where(chosen[:, :, None], accumulated, jnp.float32(0.0))
    padded = jnp.concatenate([retained, tail_zeros], axis=1)
    picked = jax.vmap(lambda source, firsts: jax.vmap(lambda first: window(source, first))(firsts))(
        padded, starts
    )
    in_region = slot_ids[None, None, :] < region_sizes[:, :, None]
    contribution = jnp.where(in_region[:, :, :, None], picked, jnp.float32(0.0))
    summed = lax.psum_scatter(contribution, "dp", scatter_dimension=1, tiled=True)[:, 0]
    my_size = lax.dynamic_index_in_dim(region_sizes, my_index, axis=1, keepdims=False)
    my_start = lax.dynamic_index_in_dim(starts, my_index, axis=1, keepdims=False)
    mine_valid = slot_ids[None, :] < my_size[:, None]
    padded_params = jnp.concatenate([params, tail_zeros], axis=1)
    old_param = jax.vmap(window)(padded_params, my_start)
    new_mom = jnp.where(
        mine_valid[:, :, None], decay_rate * momentum[:, 0] + summed, jnp.float32(0.0)
    )
    region_params = jnp.where(
        mine_valid[:, :, None], old_param - learn_rate * new_mom, jnp.float32(0.0)
    )
    everyone = lax.all_gather(region_params, "dp", axis=1, tiled=True)
    owner_all = jnp.sum((starts[:, None, 1:] <= blocks[None, :, None]).astype(jnp.int32), axis=2)
    where_row = (
        owner_all * rows_max + blocks[None, :] - jnp.take_along_axis(starts, owner_all, axis=1)
    )
    new_params = jnp.take_along_axis(everyone, where_row[:, :, None], axis=1)
    return (new_residual[None], new_mom[:, None], new_params)


def solution(mesh):
    placed = (
        P("dp", "grp", None, None),
        P("dp", "grp", None, None),
        P("grp", None, None),
        P("grp", "dp", None, None),
        P("dp", "grp", None),
        P("dp", "grp"),
        P("grp", None),
    )
    return jax.shard_map(
        on_device,
        mesh=mesh,
        in_specs=placed,
        out_specs=(P("dp", "grp", None, None), P("grp", "dp", None, None), P("grp", None, None)),
        check_vma=False,
    )
```

profile of v0, /device:TPU:1, one launch (start us, length us, event | category | flops | bytes accessed | tf_op | source)
XLA Modules:
  0.0 386.1 jit_solution(10294622990822975371)
XLA Ops:
  7.2 0.0 all-reduce.7.cloned.1.call-start
  7.2 0.7 iota_compare_fusion.3
  7.9 0.8 fusion.2
  8.8 0.5 copy.37
  9.2 0.8 copy.41
  10.0 0.9 reduce_window_sum.11
  10.9 0.7 fusion.16
  11.6 0.1 reshape.141
  11.7 0.3 iota_compare_fusion
  12.0 18.2 %bitcast_select_fusion = f32[2,2048,128]{2,0,1:T(2,128)S(1)} fusion(pred[2,2048]{0,1:T(8,128)(4,1)S(1)} %copy.37, bf16[1,2,2048,128]{3,2,1,0:T(8,128)(2,1)} %param.7, f32[1,2,2048,128]{3,2,1,0:T(8,128)} %param.8), kind=kLoop, calls=%fused_computation.5 | loop fusion | flops 1572864 | bytes 5246976 | tf_op jit(solution)/shard_map/jit(_where)/select_n | solution.py:30
  30.3 1.0 concatenate.12
  31.3 10.4 %gather_fusion = f32[128,63,128]{2,0,1:T(8,128)} fusion(f32[2,2111,128]{2,0,1:T(2,128)S(1)} %concatenate.12, s32[128]{0:T(128)S(1)} %reshape.141), kind=kCustom, calls=%fused_computation | custom fusion | bytes 8259072 | tf_op jit(solution)/shard_map/vmap(vmap())/gather | solution.py:28
  41.7 9.8 %copy_select_fusion = f32[2,64,63,128]{3,0,2,1:T(2,128)} fusion(f32[2,64,63,128]{3,1,0,2:T(8,128)} %bitcast.44, pred[2,64,63]{0,2,1:T(8,128)(4,1)S(1)} %iota_compare_fusion), kind=kLoop, calls=%fused_computation.4 | loop fusion | flops 1032192 | bytes 8265600 | tf_op jit(solution)/shard_map/jit(_where)/select_n | solution.py:36
  51.4 0.0 copy-start.2
  51.4 0.0 all-reduce.7.cloned.1.call-update
  51.5 0.2 all-gather.2.cloned.1.call-start
  51.7 1.3 copy-done.2
  53.0 7.6 %copy.45 = f32[2,2048,128]{2,0,1:T(2,128)S(1)} copy(f32[2,2048,128]{2,1,0:T(8,128)S(1)} %copy-done.2) | data formatting | bytes 4194304 | tf_op args[2]
  60.6 0.0 copy-start.5
  60.6 0.0 copy-start.4
  60.6 0.0 copy-start.3
  60.6 1.0 concatenate.14
  61.7 0.0 copy-done.5
  61.7 0.6 dynamic-slice
  62.3 0.0 copy-done.4
  62.3 0.2 dynamic-slice_reduce_fusion
  62.5 0.8 gather_fusion.2
  63.4 185.8 %all-reduce.7.cloned.1.call-done = f32[2,64,63,128]{3,0,2,1:T(2,128)} async-done(((f32[2,64,63,128]{3,0,2,1:T(2,128)}), f32[2,64,63,128]{3,0,2,1:T(2,128)}) %all-reduce.7.cloned.1.call-update) | async-done | bytes 4128784
  249.2 0.0 copy-done.3
  249.2 2.3 fusion.5
  251.4 0.0 all-gather.2.cloned.1.call-update
  251.5 0.1 slice.3
  251.5 0.1 copy.44
  251.6 0.7 fusion
  252.4 0.0 copy-start
  252.4 0.0 copy-start.1
  252.4 34.6 %gather_fusion.1 = s32[4096]{0:T(1024)S(1)} fusion(s32[2,64]{1,0:T(2,128)S(1)} %get-tuple-element.16, s32[4096]{0:T(1024)S(1)} %bitcast.43), kind=kCustom, calls=%fused_computation.1 | custom fusion | bytes 65536 | tf_op jit(solution)/shard_map/jit(take_along_axis)/gather | solution.py:52
  287.0 0.0 copy-done
  287.0 0.0 copy-done.1
  287.0 18.2 %broadcast_select_fusion = f32[1,2,2048,128]{3,1,2,0:T(2,128)S(1)} fusion(pred[2,2048]{0,1:T(8,128)(4,1)S(1)} %copy.37, bf16[1,2,2048,128]{3,2,1,0:T(8,128)(2,1)S(1)} %copy-done.1, f32[1,2,2048,128]{3,2,1,0:T(8,128)S(1)} %copy-done), kind=kLoop, calls=%fused_computation.8 | loop fusion | flops 1572864 | bytes 5246976 | tf_op jit(solution)/shard_map/jit(_where)/select_n | solution.py:22
  305.3 1.5 copy.47
  306.8 0.1 compare_and_fusion
  306.9 1.6 broadcast_select_fusion.2
  308.5 0.7 copy.48
  309.2 22.9 %all-gather.2.cloned.1.call-done = f32[2,4032,128]{2,0,1:T(2,128)} async-done(((f32[2,63,128]{2,0,1:T(2,128)}), f32[2,4032,128]{2,0,1:T(2,128)}) %all-gather.2.cloned.1.call-update) | async-done | bytes 4128784 | tf_op jit(solution)/shard_map/all_gather | solution.py:49
  332.1 4.4 %copy.46 = f32[2,4032,128]{2,1,0:T(8,128)} copy(f32[2,4032,128]{2,0,1:T(2,128)} %all-gather.2.cloned.1.call-done) | data formatting | bytes 8257536 | tf_op jit(solution)/shard_map/all_gather | solution.py:49
  336.4 40.5 %gather_fusion.3 = f32[4096,128]{1,0:T(8,128)S(1)} fusion(f32[2,4032,128]{2,1,0:T(8,128)} %copy.46, s32[4096]{0:T(1024)S(1)} %bitcast.42), kind=kCustom, calls=%fused_computation.3 | custom fusion | bytes 4227072 | tf_op jit(solution)/shard_map/jit(take_along_axis)/gather | solution.py:54
  377.0 2.2 broadcast_select_fusion.1
  (7 shorter events, 0.1 us)
Async XLA Ops:
  7.2 242.0 %all-reduce.7.cloned.1.call-start = ((), (), s32[]{:S(2)}) async-start(), calls=%async_computation.1 | async-start | bytes 8257536
  51.4 1.6 copy-start.2
  51.5 280.6 %all-gather.2.cloned.1.call-start = ((), (), s32[]{:S(2)}) async-start(), calls=%async_computation | async-start | bytes 4193280 | tf_op jit(solution)/shard_map/all_gather | solution.py:49
  60.6 1.1 copy-start.5
  60.6 1.7 copy-start.4
  60.6 188.5 %copy-start.3 = (f32[2,1,63,128]{3,1,2,0:T(1,128)S(1)}, f32[2,1,63,128]{3,1,2,0:T(1,128)}, u32[]{:S(2)}) copy-start(f32[2,1,63,128]{3,1,2,0:T(1,128)} %param.10) | copy-start | bytes 193540
  252.4 34.6 %copy-start = (f32[1,2,2048,128]{3,2,1,0:T(8,128)S(1)}, f32[1,2,2048,128]{3,2,1,0:T(8,128)}, u32[]{:S(2)}) copy-start(f32[1,2,2048,128]{3,2,1,0:T(8,128)} %param.8) | copy-start | bytes 6291460
  252.4 34.6 %copy-start.1 = (bf16[1,2,2048,128]{3,2,1,0:T(8,128)(2,1)S(1)}, bf16[1,2,2048,128]{3,2,1,0:T(8,128)(2,1)}, u32[]{:S(2)}) copy-start(bf16[1,2,2048,128]{3,2,1,0:T(8,128)(2,1)} %param.7) | copy-start | bytes 3145732
Sparse Core Ops, SparseCore 0:
  51.6 197.5 all-reduce.6
  252.4 79.6 all-gather.1
where the time goes:
time: 387 us; the launch traced here: 386 us
  waiting for transfers between devices  209 us (54%)
  local copies, waits for them, and re-layouts  106 us (27%)
  other arithmetic  56.9 us (15%)
  between operations  14.3 us (4%)
    unnamed x3, waiting for transfers between devices  186 us
    gather x1, local copies, waits for them, and re-layouts, on_device(): new_params = jnp.take_along_axis(everyone, where_row[:, :, None], axis=1)  40.5 us
    gather x3, local copies, waits for them, and re-layouts, on_device(): jnp.take_along_axis(starts, owner_all, axis=1)  34.6 us
    all_gather x1, waiting for transfers between devices, on_device(): everyone = lax.all_gather(region_params, 'dp', axis=1, tiled=True)  22.9 us
    select_n x1, other arithmetic, on_device(): new_residual = jnp.where(chosen[:, :, None], jnp.float32(0.0), accumulated)  18.2 us
    select_n x1, other arithmetic, on_device(): retained = jnp.where(chosen[:, :, None], accumulated, jnp.float32(0.0))  18.2 us
    unnamed x19, local copies, waits for them, and re-layouts  12.4 us
    gather x3, local copies, waits for them, and re-layouts, window(): return lax.dynamic_slice_in_dim(source, first, rows_max, 0)  11.3 us
  transfers between devices with their start and end apart: 2, of which 2 were waited for; matrix products, arithmetic and copies ran while one was open for 18% of the time, Pallas kernels for 0%

commit v1 on v0

v1 whole, which is shorter than its diff:
```python
import functools
import heapq

import jax
import jax.numpy as jnp
from jax import lax
from jax.experimental import pallas as pl
from jax.experimental.pallas import tpu as pltpu
from jax.sharding import PartitionSpec as P

decay_rate = 0.9
learn_rate = 0.1

NZ, NY = 8, 4
SLOTS = NZ * NY
ROWS = 160
MESH = pl.DeviceIdType.MESH
CHUNKS = 4


def z_first(rows):
    children = {}
    for ry in range(NY):
        for rz in range(NZ):
            children[(rz, ry)] = []
    for a, b in ((0, 1), (1, 2), (2, 3), (3, 4), (0, 7), (7, 6), (6, 5)):
        children[(a, 0)].append((b, 0))
    for rz in range(NZ):
        for a, b in ((0, 1), (1, 2), (0, 3)):
            children[(rz, a)].append((rz, b))
    return rows, children


def y_first(rows):
    children = {}
    for ry in range(NY):
        for rz in range(NZ):
            children[(rz, ry)] = []
    for a, b in ((0, 1), (1, 2), (0, 3)):
        children[(0, a)].append((0, b))
    for ry in range(NY):
        for a, b in ((0, 1), (1, 2), (2, 3), (3, 4), (0, 7), (7, 6), (6, 5)):
            children[(a, ry)].append((b, ry))
    return rows, children


FLOWS = (z_first((0, 96)), y_first((96, 160)))


def schedule(flows):
    def height(children, node):
        return 1 + max((height(children, c) for c in children[node]), default=0)

    heap = [(0.0, f, (0, 0)) for f in range(len(flows))]
    free = {"z": 0.0, "y": 0.0}
    now, order = 0.0, []
    while heap:
        at, f, node = heapq.heappop(heap)
        now = max(now, at) + 0.05
        (first, last), children = flows[f]
        kids = sorted(children[node], key=lambda c: -height(children, c))
        order.append((f, node, kids))
        for kid in kids:
            now += 0.07
            axis = "z" if kid[1] == node[1] else "y"
            free[axis] = max(free[axis], now) + (last - first) * 512 / 105e3
            heapq.heappush(heap, (free[axis] + 1.9, f, kid))
    return order


ORDER = schedule(FLOWS)


def slot_of(node):
    return node[0] * NY + node[1]


def gather_kernel(
    idx_s, cnt_s, idx_v, grads, residual, momentum,
    everyone, acc_out,
    gbuf, rbuf, abuf, send_sem, recv_sem, pair_send, pair_recv, in_sem, mom_sem, out_sem,
):
    me = lax.axis_index("dp")
    core = lax.rem(me, 2)
    y = lax.rem(lax.div(me, 2), NY)
    z = lax.div(me, 2 * NY)
    turn = 1 - 2 * core

    def at(dz, dy):
        return (lax.rem(z + turn * dz + NZ, NZ) * NY + lax.rem(y + turn * dy + NY, NY)) * 2 + core

    sibling = me + turn
    targets = {(1, 0): at(1, 0), (7, 0): at(-1, 0), (0, 1): at(0, 1), (0, 3): at(0, -1)}

    barrier = pltpu.get_barrier_semaphore()
    for t in list(targets.values()) + [sibling]:
        pl.semaphore_signal(barrier, inc=1, device_id={"dp": t}, device_id_type=MESH)

    nb = residual.shape[2]
    part = nb // CHUNKS
    for b in range(2):
        pltpu.make_async_copy(
            momentum.at[b, 0], everyone.at[0, 0, pl.ds(64 * b, 63)], mom_sem.at[b]
        ).start()
    loads = []
    for b in range(2):
        for k in range(CHUNKS):
            span = pl.ds(k * part, part)
            j = b * CHUNKS + k
            g = pltpu.make_async_copy(grads.at[0, b, span], gbuf.at[b, span], in_sem.at[0, j])
            r = pltpu.make_async_copy(residual.at[0, b, span], rbuf.at[b, span], in_sem.at[1, j])
            g.start()
            r.start()
            loads.append((g, r))
    for b in range(2):
        everyone[0, 0, pl.ds(64 * b + 63, 1), :] = jnp.zeros((1, 128), jnp.float32)
        everyone[0, 0, pl.ds(64 * b + 63, 1), 0:16] = idx_v[0, pl.ds(b, 1), :].astype(jnp.float32)
    stores = []
    for b in range(2):
        for k in range(CHUNKS):
            j = b * CHUNKS + k
            span = pl.ds(k * part, part)
            g, r = loads[j]
            g.wait()
            r.wait()
            abuf[b, span, :] = rbuf[b, span, :] + gbuf[b, span, :].astype(jnp.float32)
            s = pltpu.make_async_copy(abuf.at[b, span], acc_out.at[b, span], out_sem.at[j])
            s.start()
            stores.append(s)
    for b in range(2):
        for i in range(16):
            row = abuf[b, pl.ds(idx_s[0, b, i], 1), :]
            everyone[0, 0, pl.ds(128 + 16 * b + i, 1), :] = jnp.where(
                i < cnt_s[0, b], row, jnp.float32(0.0)
            )
    for b in range(2):
        pltpu.make_async_copy(
            momentum.at[b, 0], everyone.at[0, 0, pl.ds(64 * b, 63)], mom_sem.at[b]
        ).wait()
    pl.semaphore_wait(barrier, 5)

    def piece(f, node, side=0):
        first, last = FLOWS[f][0]
        return everyone.at[side, slot_of(node), pl.ds(first, last - first)]

    def hop(f, node, kid):
        step = ((kid[0] - node[0]) % NZ, (kid[1] - node[1]) % NY)
        return pltpu.make_async_remote_copy(
            src_ref=piece(f, node),
            dst_ref=piece(f, kid),
            send_sem=send_sem.at[f, slot_of(kid)],
            recv_sem=recv_sem.at[f, slot_of(kid)],
            device_id={"dp": targets[step]},
            device_id_type=MESH,
        )

    def across(f, node):
        return pltpu.make_async_remote_copy(
            src_ref=piece(f, node),
            dst_ref=piece(f, node, 1),
            send_sem=pair_send.at[f, slot_of(node)],
            recv_sem=pair_recv.at[f, slot_of(node)],
            device_id={"dp": sibling},
            device_id_type=MESH,
        )

    parent = {(f, kid): node for f, node, kids in ORDER for kid in kids}
    for f, node, kids in ORDER:
        if node != (0, 0):
            hop(f, parent[(f, node)], node).wait_recv()
        for kid in kids:
            hop(f, node, kid).start()
        across(f, node).start()
    for f, node, kids in ORDER:
        across(f, node).wait_recv()
    for f, node, kids in ORDER:
        for kid in kids:
            hop(f, node, kid).wait_send()
        across(f, node).wait_send()
    for s in stores:
        s.wait()


def update_kernel(
    sizes, idx_own, cnt, everyone, acc, params,
    new_residual, new_momentum, new_params,
    pbuf, nm, lists_v, lists_s, zero_row, res_sem, row_sem, in_sem, out_sem, list_sem,
):
    me = lax.axis_index("dp")
    core = lax.rem(me, 2)
    y = lax.rem(lax.div(me, 2), NY)
    z = lax.div(me, 2 * NY)
    nb = params.shape[1]
    move = pltpu.make_async_copy(acc, new_residual.at[0], res_sem)
    move.start()
    load = pltpu.make_async_copy(params, pbuf, in_sem)
    load.start()
    zero_row[...] = jnp.zeros_like(zero_row)

    def place_of(o):
        oz, oy, oc = lax.shift_right_logical(o, 3), lax.shift_right_logical(o, 1) & 3, o & 1
        turn = 1 - 2 * oc
        slot = ((turn * (z - oz)) & (NZ - 1)) * NY + ((turn * (y - oy)) & (NY - 1))
        return (oc + core) & 1, slot

    def read_list(o, carry):
        side, slot = place_of(o)
        for b in range(2):
            lists_v[b, pl.ds(o, 1), :] = everyone[side, slot, pl.ds(64 * b + 63, 1), :].astype(jnp.int32)
        return carry

    lax.fori_loop(0, 64, read_list, 0, unroll=8)
    fetch = pltpu.make_async_copy(lists_v, lists_s, list_sem)
    fetch.start()

    def place(o, carry):
        s0, s1, m0, m1 = carry
        side, slot = place_of(o)
        nm[0, pl.ds(s0, 64), :] = decay_rate * everyone[side, slot, 0:64, :]
        nm[1, pl.ds(s1, 64), :] = decay_rate * everyone[side, slot, 64:128, :]
        m0 = jnp.where(o == me, s0, m0)
        m1 = jnp.where(o == me, s1, m1)
        return s0 + sizes[0, o], s1 + sizes[1, o], m0, m1

    zero = jnp.int32(0)
    _, _, m0, m1 = lax.fori_loop(0, 64, place, (zero, zero, zero, zero), unroll=4)
    fetch.wait()

    def add(o, carry):
        side, slot = place_of(o)
        rows = []
        for b in range(2):
            for i in range(16):
                j = lists_s[b, o, i]
                rows.append((b, j, nm[b, pl.ds(j, 1), :] + everyone[side, slot, pl.ds(128 + 16 * b + i, 1), :]))
        for b, j, row in rows:
            nm[b, pl.ds(j, 1), :] = row
        return carry

    lax.fori_loop(0, 64, add, 0, unroll=2)
    load.wait()
    part = nb // CHUNKS
    outs = []
    for b in range(2):
        for k in range(CHUNKS):
            span = pl.ds(k * part, part)
            pbuf[b, span, :] = pbuf[b, span, :] - learn_rate * nm[b, span, :]
            out = pltpu.make_async_copy(pbuf.at[b, span], new_params.at[b, span], out_sem.at[b * CHUNKS + k])
            out.start()
            outs.append(out)
    rows = new_momentum.shape[2]
    for b, first in ((0, m0), (1, m1)):
        mine = nm[b, pl.ds(first, rows), :]
        inside = lax.broadcasted_iota(jnp.int32, (rows, 128), 0) < sizes[b, me]
        new_momentum[b, 0] = jnp.where(inside, mine, jnp.float32(0.0))
    move.wait()

    def clear(b, i):
        return pltpu.make_async_copy(
            zero_row, new_residual.at[0, b, pl.ds(idx_own[0, b, i], 1)], row_sem.at[b, i]
        )

    for b in range(2):
        for i in range(16):

            @pl.when(i < cnt[0, b])
            def _():
                clear(b, i).start()

    for b in range(2):
        for i in range(16):

            @pl.when(i < cnt[0, b])
            def _():
                clear(b, i).wait()

    for out in outs:
        out.wait()


def on_device(grads, residual, params, momentum, indices, counts, region_sizes):
    nb = grads.shape[2]
    any_space = pl.BlockSpec(memory_space=pl.ANY)
    vmem = pl.BlockSpec(memory_space=pltpu.VMEM)
    smem = pl.BlockSpec(memory_space=pltpu.SMEM)
    dma = pltpu.SemaphoreType.DMA
    everyone, acc = pl.pallas_call(
        gather_kernel,
        out_shape=(
            jax.ShapeDtypeStruct((2, SLOTS, ROWS, 128), jnp.float32),
            jax.ShapeDtypeStruct((2, nb, 128), jnp.float32),
        ),
        in_specs=[smem, smem, vmem, any_space, any_space, any_space],
        out_specs=(vmem, any_space),
        scratch_shapes=[
            pltpu.VMEM((2, nb, 128), jnp.bfloat16),
            pltpu.VMEM((2, nb, 128), jnp.float32),
            pltpu.VMEM((2, nb, 128), jnp.float32),
            dma((len(FLOWS), SLOTS)),
            dma((len(FLOWS), SLOTS)),
            dma((len(FLOWS), SLOTS)),
            dma((len(FLOWS), SLOTS)),
            dma((2, 2 * CHUNKS)),
            dma((2,)),
            dma((2 * CHUNKS,)),
        ],
        compiler_params=pltpu.CompilerParams(
            collective_id=0, has_side_effects=True, vmem_limit_bytes=32 << 20
        ),
        name="gather",
    )(indices, counts, indices, grads, residual, momentum)
    return pl.pallas_call(
        update_kernel,
        out_shape=(
            jax.ShapeDtypeStruct((1, 2, nb, 128), jnp.float32),
            jax.ShapeDtypeStruct(momentum.shape, jnp.float32),
            jax.ShapeDtypeStruct(params.shape, jnp.float32),
        ),
        in_specs=[smem, smem, smem, vmem, any_space, any_space],
        out_specs=(any_space, vmem, any_space),
        scratch_shapes=[
            pltpu.VMEM((2, nb, 128), jnp.float32),
            pltpu.VMEM((2, nb + 64, 128), jnp.float32),
            pltpu.VMEM((2, 64, 128), jnp.int32),
            pltpu.SMEM((2, 64, 128), jnp.int32),
            pltpu.VMEM((1, 128), jnp.float32),
            dma,
            dma((2, 16)),
            dma,
            dma((2 * CHUNKS,)),
            dma,
        ],
        compiler_params=pltpu.CompilerParams(vmem_limit_bytes=32 << 20),
        name="update",
    )(region_sizes, indices, counts, everyone, acc, params)


def solution(mesh):
    placed = (
        P("dp", "grp", None, None),
        P("dp", "grp", None, None),
        P("grp", None, None),
        P("grp", "dp", None, None),
        P("dp", "grp", None),
        P("dp", "grp"),
        P("grp", None),
    )
    return jax.shard_map(
        on_device,
        mesh=mesh,
        in_specs=placed,
        out_specs=(P("dp", "grp", None, None), P("grp", "dp", None, None), P("grp", None, None)),
        check_vma=False,
    )
```

time: 387 us -> 50.2 us (0.13)
  waiting for transfers between devices: 209 us -> 0 us
  local copies, waits for them, and re-layouts: 106 us -> 5.7 us
  other arithmetic: 56.9 us -> 0 us
  Pallas kernels: 0 us -> 43.6 us
  between operations: 14.3 us -> 0.68 us
    unnamed x3 -> x0, waiting for transfers between devices: 186 us -> none
    gather x7 -> x0, local copies, waits for them, and re-layouts: 86.4 us -> none  [the longest x1 40.5 us: on_device(): new_params = jnp.take_along_axis(everyone, where_row[:, :, None], axis=1)]
    select_n x6 -> x0, other arithmetic: 52.4 us -> none  [the longest x1 18.2 us: on_device(): new_residual = jnp.where(chosen[:, :, None], jnp.float32(0.0), accumulated)]
    pallas_call x0 -> x2, Pallas kernels: none -> 43.6 us  [the longest x1 35.5 us: on_device(): pl.pallas_call(gather_kernel, out_shape=(jax.ShapeDtypeStruct((2, SLOTS,...]
    all_gather x1 -> x0, waiting for transfers between devices: 22.9 us -> none  [on_device(): everyone = lax.all_gather(region_params, 'dp', axis=1, tiled=True)]
    unnamed x19 -> x13, local copies, waits for them, and re-layouts: 12.4 us -> 5 us
    all_gather x1 -> x0, local copies, waits for them, and re-layouts: 4.37 us -> none  [on_device(): everyone = lax.all_gather(region_params, 'dp', axis=1, tiled=True)]
  transfers between devices with their start and end apart: 2 -> 0, of which waited for: 2 -> 0; matrix products, arithmetic and copies ran while one was open for 18% -> 0% of each run, Pallas kernels for 0% -> 0%
where the time goes in v1:
time: 50.2 us; the launch traced here: 49.9 us
  Pallas kernels  43.6 us (87%)
  local copies, waits for them, and re-layouts  5.7 us (11%)
  between operations  0.68 us (1%)
    pallas_call x1, Pallas kernels, on_device(): pl.pallas_call(gather_kernel, out_shape=(jax.ShapeDtypeStruct((2, SLOTS,...  35.5 us
    pallas_call x1, Pallas kernels, on_device(): pl.pallas_call(update_kernel, out_shape=(jax.ShapeDtypeStruct((1, 2, nb,...  8.1 us
    unnamed x13, local copies, waits for them, and re-layouts  5 us

profile of v1, /device:TPU:1, one launch (start us, length us, event | category | flops | bytes accessed | tf_op | source)
XLA Modules:
  0.0 49.9 jit_solution(17073303544056462351)
XLA Ops:
  0.6 0.0 copy-start.5
  0.6 0.8 %copy.10.momentum = f32[2,1,63,128]{3,2,1,0:T(8,128)S(1)} copy(f32[2,1,63,128]{3,1,2,0:T(1,128)} %param.10) | data formatting | bytes 129024 | tf_op args[3]
  1.5 0.0 copy-start
  1.5 1.6 %copy-done = f32[1,2,2048,128]{3,2,1,0:T(8,128)S(1)} copy-done((f32[1,2,2048,128]{3,2,1,0:T(8,128)S(1)}, f32[1,2,2048,128]{3,2,1,0:T(8,128)}, u32[]{:S(2)}) %copy-start) | copy-done | bytes 2097176
  3.1 0.0 copy-start.2
  3.1 1.2 %copy-done.2 = bf16[1,2,2048,128]{3,2,1,0:T(8,128)(2,1)S(1)} copy-done((bf16[1,2,2048,128]{3,2,1,0:T(8,128)(2,1)S(1)}, bf16[1,2,2048,128]{3,2,1,0:T(8,128)(2,1)}, u32[]{:S(2)}) %copy-start.2) | copy-done | bytes 1048600
  4.3 0.0 copy-start.3
  4.3 0.7 %copy-done.3 = s32[1,2,16]{2,1,0:T(2,128)S(1)} copy-done((s32[1,2,16]{2,1,0:T(2,128)S(1)}, s32[1,2,16]{2,1,0:T(2,128)}, u32[]{:S(2)}) %copy-start.3) | copy-done | bytes 152
  5.0 0.0 copy-start.4
  5.0 0.7 %copy-done.4 = s32[1,2]{1,0:T(1,128)S(1)} copy-done((s32[1,2]{1,0:T(1,128)S(1)}, s32[1,2]{1,0:T(1,128)}, u32[]{:S(2)}) %copy-start.4) | copy-done | bytes 32
  5.6 0.0 copy-start.1
  5.6 35.5 %gather.1 = (f32[2,32,160,128]{3,2,1,0:T(8,128)S(1)}, f32[2,2048,128]{2,1,0:T(8,128)S(1)}) custom-call(s32[1,2,16]{2,1,0:T(2,128)S(1)} %copy-done.3, s32[1,2]{1,0:T(1,128)S(1)} %copy-done.4, s32[1,2,16]{2,1,0:T(2,128)S(1)} %copy-done.3, bf16[1,2,2048,128]{3,2,1,0:T(8,128)(2,1)S(1)} %copy-done.2, f32[1,2,2048,128]{3,2,1,0:T(8,128)S(1)} %copy-done, ...), custom_call_target="tpu_custom_call" | custom-call | tf_op jit(solution)/shard_map/gather/pallas_call | solution.py:287
  41.1 0.0 copy-done.5
  41.1 0.0 copy-done.1
  41.1 8.1 %update.1 = (f32[1,2,2048,128]{3,2,1,0:T(8,128)}, f32[2,1,63,128]{3,2,1,0:T(8,128)S(1)}, f32[2,2048,128]{2,1,0:T(8,128)}) custom-call(s32[2,64]{1,0:T(2,128)S(1)} %copy-done.5, s32[1,2,16]{2,1,0:T(2,128)S(1)} %copy-done.3, s32[1,2]{1,0:T(1,128)S(1)} %copy-done.4, f32[2,32,160,128]{3,2,1,0:T(8,128)S(1)} %get-tuple-element.5.everyone, ...), custom_call_target="tpu_custom_call" | custom-call | tf_op jit(solution)/shard_map/update/pallas_call | solution.py:312
  49.2 0.7 %copy.11 = f32[2,1,63,128]{3,1,2,0:T(1,128)} copy(f32[2,1,63,128]{3,2,1,0:T(8,128)S(1)} %get-tuple-element.8) | data formatting | bytes 129024 | tf_op jit(solution)/shard_map/update/pallas_call | solution.py:312
Async XLA Ops:
  0.6 40.5 %copy-start.5 = (s32[2,64]{1,0:T(2,128)S(1)}, s32[2,64]{1,0:T(2,128)}, u32[]{:S(2)}) copy-start(s32[2,64]{1,0:T(2,128)} %sizes.1) | copy-start | bytes 1540
  1.5 1.6 %copy-start = (f32[1,2,2048,128]{3,2,1,0:T(8,128)S(1)}, f32[1,2,2048,128]{3,2,1,0:T(8,128)}, u32[]{:S(2)}) copy-start(f32[1,2,2048,128]{3,2,1,0:T(8,128)} %residual.1) | copy-start | bytes 6291460
  3.1 1.2 %copy-start.2 = (bf16[1,2,2048,128]{3,2,1,0:T(8,128)(2,1)S(1)}, bf16[1,2,2048,128]{3,2,1,0:T(8,128)(2,1)}, u32[]{:S(2)}) copy-start(bf16[1,2,2048,128]{3,2,1,0:T(8,128)(2,1)} %grads.1) | copy-start | bytes 3145732
  4.3 0.7 %copy-start.3 = (s32[1,2,16]{2,1,0:T(2,128)S(1)}, s32[1,2,16]{2,1,0:T(2,128)}, u32[]{:S(2)}) copy-start(s32[1,2,16]{2,1,0:T(2,128)} %idx_own.1) | copy-start | bytes 388
  5.0 0.7 %copy-start.4 = (s32[1,2]{1,0:T(1,128)S(1)}, s32[1,2]{1,0:T(1,128)}, u32[]{:S(2)}) copy-start(s32[1,2]{1,0:T(1,128)} %cnt.1) | copy-start | bytes 28
  5.6 35.5 %copy-start.1 = (f32[2,2048,128]{2,1,0:T(8,128)S(1)}, f32[2,2048,128]{2,1,0:T(8,128)}, u32[]{:S(2)}) copy-start(f32[2,2048,128]{2,1,0:T(8,128)} %params.1) | copy-start | bytes 6291460

commit v2 on v1

v2 whole, which is shorter than its diff:
```python
import functools
import heapq

import jax
import jax.numpy as jnp
from jax import lax
from jax.experimental import pallas as pl
from jax.experimental.pallas import tpu as pltpu
from jax.sharding import PartitionSpec as P

decay_rate = 0.9
learn_rate = 0.1

NZ, NY = 8, 4
SLOTS = NZ * NY
ROWS = 160
MESH = pl.DeviceIdType.MESH
CHUNKS = 4
PITCH = 2048 + 64


Z_TREES = {
    4: ((0, 1), (1, 2), (2, 3), (3, 4), (0, 7), (7, 6), (6, 5)),
    3: ((0, 1), (1, 2), (2, 3), (2, 4), (0, 7), (7, 6), (6, 5)),
    2: ((0, 1), (0, 2), (2, 3), (2, 4), (0, 7), (0, 6), (6, 5)),
    1: ((0, 1), (0, 2), (0, 3), (0, 4), (0, 7), (0, 6), (0, 5)),
}
Y_TREES = {2: ((0, 1), (1, 2), (0, 3)), 1: ((0, 1), (0, 2), (0, 3))}

FLOWS = (
    (0, 96, True, 3, 1, False),
    (96, 160, False, 3, 1, True),
)


def tree_of(flow):
    _, _, along_z, zt, yt, _ = flow
    children = {(rz, ry): [] for rz in range(NZ) for ry in range(NY)}
    for a, b in Z_TREES[zt]:
        for ry in range(1 if along_z else NY):
            children[(a, ry)].append((b, ry))
    for a, b in Y_TREES[yt]:
        for rz in range(NZ if along_z else 1):
            children[(rz, a)].append((rz, b))
    return children


TREES = tuple(tree_of(flow) for flow in FLOWS)


def step_of(node, kid):
    dz, dy = (kid[0] - node[0]) % NZ, (kid[1] - node[1]) % NY
    return (dz if 2 * dz <= NZ else dz - NZ), (dy if 2 * dy <= NY else dy - NY)


STEPS = tuple(sorted({step_of(n, k) for t in TREES for n, kids in t.items() for k in kids}))
LATENCY, PER_HOP, PICKS = 1.6, 0.65, 1.5


def schedule():
    def height(f, node):
        return 1 + max((height(f, c) for c in TREES[f][node]), default=0)

    heap = [(PICKS if FLOWS[f][5] else 0.0, f, (0, 0)) for f in range(len(FLOWS))]
    free = {"z": 0.0, "y": 0.0}
    now, order = 0.0, []
    while heap:
        at, f, node = heapq.heappop(heap)
        now = max(now, at) + 0.05
        kids = sorted(TREES[f][node], key=lambda c: -height(f, c))
        order.append((f, node, kids))
        for kid in kids:
            now += 0.07
            dz, dy = step_of(node, kid)
            axis, hops = ("z", abs(dz)) if dz else ("y", abs(dy))
            free[axis] = max(free[axis], now) + hops * (FLOWS[f][1] - FLOWS[f][0]) * 512 / 105e3
            heapq.heappush(heap, (free[axis] + LATENCY + hops * PER_HOP, f, kid))
    return order


ORDER = schedule()


def slot_of(node):
    return node[0] * NY + node[1]


def gather_kernel(
    idx, cnt, grads, residual, momentum,
    everyone, acc_out,
    idx_s, cnt_s, idx_v, gbuf, rbuf,
    send_sem, recv_sem, pair_send, pair_recv, in_sem, mom_sem, small_sem,
):
    me = lax.axis_index("dp")
    core = lax.rem(me, 2)
    y = lax.rem(lax.div(me, 2), NY)
    z = lax.div(me, 2 * NY)
    turn = 1 - 2 * core

    def at(dz, dy):
        return (lax.rem(z + turn * dz + NZ, NZ) * NY + lax.rem(y + turn * dy + NY, NY)) * 2 + core

    sibling = me + turn
    targets = {step: at(*step) for step in STEPS}

    barrier = pltpu.get_barrier_semaphore()
    for t in [at(-dz, -dy) for dz, dy in STEPS] + [sibling]:
        pl.semaphore_signal(barrier, inc=1, device_id={"dp": t}, device_id_type=MESH)

    nb = residual.shape[2]
    part = nb // CHUNKS
    small = [
        pltpu.make_async_copy(idx, idx_v, small_sem.at[0]),
        pltpu.make_async_copy(idx, idx_s, small_sem.at[1]),
        pltpu.make_async_copy(cnt, cnt_s, small_sem.at[2]),
    ]
    for b in range(2):
        small.append(
            pltpu.make_async_copy(
                momentum.at[b, :, 0], everyone.at[0, 0, pl.ds(64 * b, 63)], mom_sem.at[b]
            )
        )
    for copy in small:
        copy.start()
    loads = []
    for b in range(2):
        for k in range(CHUNKS):
            span = pl.ds(k * part, part)
            j = b * CHUNKS + k
            g = pltpu.make_async_copy(grads.at[0, b, span], gbuf.at[b, span], in_sem.at[0, j])
            r = pltpu.make_async_copy(residual.at[0, b, span], rbuf.at[b, span], in_sem.at[1, j])
            g.start()
            r.start()
            loads.append((g, r))
    for copy in small:
        copy.wait()
    offset = PITCH * lax.broadcasted_iota(jnp.int32, (2, 16), 0)
    lists = (idx_v[0] + offset).astype(jnp.float32)
    for q in range(8):
        everyone[0, 0, 63:64, 16 * q : 16 * q + 16] = lists[q % 2 : q % 2 + 1]
    lane = lax.broadcasted_iota(jnp.int32, (1, 128), 1)
    own = lax.div(lane, 32) == lax.rem(me, 4)
    everyone[0, 0, 63:64, :] = jnp.where(own, everyone[0, 0, 63:64, :], jnp.float32(0.0))
    everyone[0, 0, 127:128, :] = jnp.zeros((1, 128), jnp.float32)

    def piece(f, node, side=0):
        first, last = FLOWS[f][:2]
        return everyone.at[side, slot_of(node), pl.ds(first, last - first)]

    def remote(src, dst, sent, received, target):
        return pltpu.make_async_remote_copy(
            src_ref=src,
            dst_ref=dst,
            send_sem=sent,
            recv_sem=received,
            device_id={"dp": target},
            device_id_type=MESH,
        )

    def hop(f, node, kid):
        return remote(
            piece(f, node),
            piece(f, kid),
            send_sem.at[f],
            recv_sem.at[f, slot_of(kid)],
            targets[step_of(node, kid)],
        )

    def across(f, node):
        return remote(piece(f, node), piece(f, node, 1), pair_send.at[f], pair_recv.at[f], sibling)

    pl.semaphore_wait(barrier, len(STEPS) + 1)

    def pass_on(f, node, kids):
        for kid in kids:
            hop(f, node, kid).start()
        across(f, node).start()

    for f, node, kids in ORDER:
        if node == (0, 0) and not FLOWS[f][5]:
            pass_on(f, node, kids)
    for b in range(2):
        for k in range(CHUNKS):
            j = b * CHUNKS + k
            span = pl.ds(k * part, part)
            g, r = loads[j]
            g.wait()
            r.wait()
            acc_out[b, span, :] = rbuf[b, span, :] + gbuf[b, span, :].astype(jnp.float32)
    for b in range(2):
        for i in range(16):
            row = acc_out[b, pl.ds(idx_s[0, b, i], 1), :]
            everyone[0, 0, pl.ds(128 + 16 * b + i, 1), :] = jnp.where(
                i < cnt_s[0, b], row, jnp.float32(0.0)
            )
    for f, node, kids in ORDER:
        if node == (0, 0) and FLOWS[f][5]:
            pass_on(f, node, kids)
    parent = {(f, kid): node for f, node, kids in ORDER for kid in kids}
    for f, node, kids in ORDER:
        if node != (0, 0):
            hop(f, parent[(f, node)], node).wait_recv()
            pass_on(f, node, kids)
    for f in range(len(FLOWS)):
        first, last = FLOWS[f][:2]
        span = pl.ds(first, last - first)
        others = everyone.at[0, pl.ds(1, SLOTS - 1), span]
        remote(others, others, send_sem.at[f], pair_recv.at[f], sibling).wait_send()
        pair = remote(everyone.at[0, :, span], everyone.at[1, :, span], pair_send.at[f], pair_recv.at[f], sibling)
        pair.wait_send()
        pair.wait_recv()


def update_kernel(
    sizes, idx_own, cnt, everyone, acc, params,
    new_residual, new_momentum, new_params,
    pbuf, nm, mine_v, lists_v, lists_s, zero_row, mom_sem, res_sem, row_sem, out_sem, list_sem,
):
    me = lax.axis_index("dp")
    core = lax.rem(me, 2)
    y = lax.rem(lax.div(me, 2), NY)
    z = lax.div(me, 2 * NY)
    nb = params.shape[1]
    move = pltpu.make_async_copy(acc, new_residual.at[0], res_sem)
    move.start()
    zero_row[...] = jnp.zeros_like(zero_row)

    def place_of(o):
        oz, oy, oc = o >> 3, (o >> 1) & 3, o & 1
        turn = 1 - 2 * oc
        slot = ((turn * (z - oz)) & (NZ - 1)) * NY + ((turn * (y - oy)) & (NY - 1))
        return (oc + core) & 1, slot

    for q in range(16):
        row = None
        for o in range(4 * q, 4 * q + 4):
            side, slot = place_of(o)
            one = everyone[side, slot, 63:64, :]
            row = one if row is None else row + one
        lists_v[q : q + 1, :] = row.astype(jnp.int32)
    fetch = pltpu.make_async_copy(lists_v, lists_s, list_sem)
    fetch.start()

    def place(o, carry):
        s0, s1, m0, m1 = carry
        side, slot = place_of(o)
        nm[pl.ds(s0, 64), :] = decay_rate * everyone[side, slot, 0:64, :]
        nm[pl.ds(s1, 64), :] = decay_rate * everyone[side, slot, 64:128, :]
        m0 = jnp.where(o == me, s0, m0)
        m1 = jnp.where(o == me, s1, m1)
        return s0 + sizes[0, o], s1 + sizes[1, o], m0, m1

    zero = jnp.int32(0)
    _, _, m0, m1 = lax.fori_loop(0, 64, place, (zero, zero + PITCH, zero, zero), unroll=4)
    fetch.wait()

    def add(q, carry):
        for k in range(4):
            side, slot = place_of(4 * q + k)
            for first in (0, 16):
                rows = []
                for i in range(first, first + 16):
                    j = lists_s[q, 32 * k + i]
                    rows.append((j, nm[pl.ds(j, 1), :] + everyone[side, slot, pl.ds(128 + i, 1), :]))
                for j, row in rows:
                    nm[pl.ds(j, 1), :] = row
        return carry

    lax.fori_loop(0, 16, add, 0)
    part = nb // CHUNKS
    outs = []
    for b in range(2):
        for k in range(CHUNKS):
            span = pl.ds(k * part, part)
            pbuf[b, span, :] = params[b, span, :] - learn_rate * nm[pl.ds(b * PITCH + k * part, part), :]
            out = pltpu.make_async_copy(pbuf.at[b, span], new_params.at[b, span], out_sem.at[b * CHUNKS + k])
            out.start()
            outs.append(out)
    rows = new_momentum.shape[1]
    for b, first in ((0, m0), (1, m1)):
        mine = nm[pl.ds(first, rows), :]
        inside = lax.broadcasted_iota(jnp.int32, (rows, 128), 0) < sizes[b, me]
        mine_v[b] = jnp.where(inside, mine, jnp.float32(0.0))
        out = pltpu.make_async_copy(mine_v.at[b], new_momentum.at[b, :, 0], mom_sem.at[b])
        out.start()
        outs.append(out)
    move.wait()

    def clear(b, i):
        return pltpu.make_async_copy(
            zero_row, new_residual.at[0, b, pl.ds(idx_own[0, b, i], 1)], row_sem.at[b, i]
        )

    for b in range(2):
        for i in range(16):

            @pl.when(i < cnt[0, b])
            def _():
                clear(b, i).start()

    for b in range(2):
        for i in range(16):

            @pl.when(i < cnt[0, b])
            def _():
                clear(b, i).wait()

    for out in outs:
        out.wait()


def on_device(grads, residual, params, momentum, indices, counts, region_sizes):
    nb = grads.shape[2]
    hbm = pl.BlockSpec(memory_space=pltpu.HBM)
    any_space = pl.BlockSpec(memory_space=pl.ANY)
    vmem = pl.BlockSpec(memory_space=pltpu.VMEM)
    smem = pl.BlockSpec(memory_space=pltpu.SMEM)
    dma = pltpu.SemaphoreType.DMA
    everyone, acc = pl.pallas_call(
        gather_kernel,
        out_shape=(
            jax.ShapeDtypeStruct((2, SLOTS, ROWS, 128), jnp.float32),
            jax.ShapeDtypeStruct((2, nb, 128), jnp.float32),
        ),
        in_specs=[hbm] * 5,
        out_specs=(vmem, vmem),
        scratch_shapes=[
            pltpu.SMEM(indices.shape, jnp.int32),
            pltpu.SMEM(counts.shape, jnp.int32),
            pltpu.VMEM(indices.shape, jnp.int32),
            pltpu.VMEM((2, nb, 128), jnp.bfloat16),
            pltpu.VMEM((2, nb, 128), jnp.float32),
            dma((len(FLOWS),)),
            dma((len(FLOWS), SLOTS)),
            dma((len(FLOWS),)),
            dma((len(FLOWS),)),
            dma((2, 2 * CHUNKS)),
            dma((2,)),
            dma((3,)),
        ],
        compiler_params=pltpu.CompilerParams(
            collective_id=0, has_side_effects=True, vmem_limit_bytes=32 << 20
        ),
        name="gather",
    )(*(pltpu.with_memory_space_constraint(a, pltpu.HBM) for a in (indices, counts, grads, residual, jnp.swapaxes(momentum, 1, 2))))
    rows = momentum.shape[2]
    new_residual, new_momentum, new_params = pl.pallas_call(
        update_kernel,
        out_shape=(
            jax.ShapeDtypeStruct((1, 2, nb, 128), jnp.float32),
            jax.ShapeDtypeStruct((2, rows, 1, 128), jnp.float32),
            jax.ShapeDtypeStruct(params.shape, jnp.float32),
        ),
        in_specs=[smem, smem, smem, vmem, vmem, vmem],
        out_specs=(any_space, any_space, any_space),
        scratch_shapes=[
            pltpu.VMEM((2, nb, 128), jnp.float32),
            pltpu.VMEM((2 * PITCH, 128), jnp.float32),
            pltpu.VMEM((2, rows, 128), jnp.float32),
            pltpu.VMEM((16, 128), jnp.int32),
            pltpu.SMEM((16, 128), jnp.int32),
            pltpu.VMEM((1, 128), jnp.float32),
            dma((2,)),
            dma,
            dma((2, 16)),
            dma((2 * CHUNKS,)),
            dma,
        ],
        compiler_params=pltpu.CompilerParams(vmem_limit_bytes=32 << 20),
        name="update",
    )(region_sizes, indices, counts, everyone, acc, params)
    return new_residual, jnp.swapaxes(new_momentum, 1, 2), new_params


def solution(mesh):
    placed = (
        P("dp", "grp", None, None),
        P("dp", "grp", None, None),
        P("grp", None, None),
        P("grp", "dp", None, None),
        P("dp", "grp", None),
        P("dp", "grp"),
        P("grp", None),
    )
    return jax.shard_map(
        on_device,
        mesh=mesh,
        in_specs=placed,
        out_specs=(P("dp", "grp", None, None), P("grp", "dp", None, None), P("grp", None, None)),
        check_vma=False,
    )
```

time: 50.2 us -> 39 us (0.78)
  local copies, waits for them, and re-layouts: 5.7 us -> 0.02 us
  Pallas kernels: 43.6 us -> 38.2 us
    unnamed x13 -> x8, local copies, waits for them, and re-layouts: 5 us -> 0.02 us
    pallas_call x1, Pallas kernels: 35.5 us -> 32.2 us  [on_device(): pl.pallas_call(gather_kernel, out_shape=(jax.ShapeDtypeStruct((2, SLOTS,...]
    pallas_call x1, Pallas kernels: 8.1 us -> 5.99 us  [on_device(): pl.pallas_call(update_kernel, out_shape=(jax.ShapeDtypeStruct((1, 2, nb,...]
    pallas_call x1 -> x0, local copies, waits for them, and re-layouts: 0.69 us -> none  [on_device(): pl.pallas_call(update_kernel, out_shape=(jax.ShapeDtypeStruct((1, 2, nb,...]
where the time goes in v2:
time: 39 us; the launch traced here: 38.9 us
  Pallas kernels  38.2 us (98%)
  between operations  0.7 us (2%)
    pallas_call x1, Pallas kernels, on_device(): pl.pallas_call(gather_kernel, out_shape=(jax.ShapeDtypeStruct((2, SLOTS,...  32.2 us
    pallas_call x1, Pallas kernels, on_device(): pl.pallas_call(update_kernel, out_shape=(jax.ShapeDtypeStruct((1, 2, nb,...  5.99 us

profile of v2, /device:TPU:1, one launch (start us, length us, event | category | flops | bytes accessed | tf_op | source)
XLA Modules:
  0.0 38.9 jit_solution(8632887795933697176)
XLA Ops:
  0.6 0.0 copy-start.2
  0.6 0.0 copy-start.1
  0.7 0.0 copy-start.3
  0.7 0.0 copy-start
  0.7 32.2 %gather.1 = (f32[2,32,160,128]{3,2,1,0:T(8,128)S(1)}, f32[2,2048,128]{2,1,0:T(8,128)S(1)}) custom-call(s32[1,2,16]{2,1,0:T(2,128)} %idx_own.1, s32[1,2]{1,0:T(1,128)} %cnt.3, bf16[1,2,2048,128]{3,2,1,0:T(8,128)(2,1)} %grads.1, f32[1,2,2048,128]{3,2,1,0:T(8,128)} %residual.1, f32[2,63,1,128]{3,2,1,0:T(1,128)} %bitcast.2), custom_call_target="tpu_custom_call" | custom-call | tf_op jit(solution)/shard_map/gather/pallas_call | solution.py:319
  32.9 0.0 copy-done.2
  32.9 0.0 copy-done.1
  32.9 0.0 copy-done.3
  32.9 0.0 copy-done
  32.9 6.0 %update.1 = (f32[1,2,2048,128]{3,2,1,0:T(8,128)}, f32[2,63,1,128]{3,2,1,0:T(1,128)}, f32[2,2048,128]{2,1,0:T(8,128)}) custom-call(s32[2,64]{1,0:T(2,128)S(1)} %copy-done.3, s32[1,2,16]{2,1,0:T(2,128)S(1)} %copy-done.1, s32[1,2]{1,0:T(1,128)S(1)} %copy-done.2, f32[2,32,160,128]{3,2,1,0:T(8,128)S(1)} %get-tuple-element.8.everyone, ...), custom_call_target="tpu_custom_call" | custom-call | tf_op jit(solution)/shard_map/update/pallas_call | solution.py:347
Async XLA Ops:
  0.6 32.2 %copy-start.2 = (s32[1,2]{1,0:T(1,128)S(1)}, s32[1,2]{1,0:T(1,128)}, u32[]{:S(2)}) copy-start(s32[1,2]{1,0:T(1,128)} %cnt.3) | copy-start | bytes 28
  0.6 32.2 %copy-start.1 = (s32[1,2,16]{2,1,0:T(2,128)S(1)}, s32[1,2,16]{2,1,0:T(2,128)}, u32[]{:S(2)}) copy-start(s32[1,2,16]{2,1,0:T(2,128)} %idx_own.1) | copy-start | bytes 388
  0.7 32.2 %copy-start.3 = (s32[2,64]{1,0:T(2,128)S(1)}, s32[2,64]{1,0:T(2,128)}, u32[]{:S(2)}) copy-start(s32[2,64]{1,0:T(2,128)} %sizes.1) | copy-start | bytes 1540
  0.7 32.2 %copy-start = (f32[2,2048,128]{2,1,0:T(8,128)S(1)}, f32[2,2048,128]{2,1,0:T(8,128)}, u32[]{:S(2)}) copy-start(f32[2,2048,128]{2,1,0:T(8,128)} %params.1) | copy-start | bytes 6291460

commit v3 on v2

--- a/solution.py
+++ b/solution.py
@@ -16,32 +16,22 @@
 ROWS = 160
 MESH = pl.DeviceIdType.MESH
 CHUNKS = 4
+TILE = 256
+PICKED = 128
 PITCH = 2048 + 64
 
 
-Z_TREES = {
-    4: ((0, 1), (1, 2), (2, 3), (3, 4), (0, 7), (7, 6), (6, 5)),
-    3: ((0, 1), (1, 2), (2, 3), (2, 4), (0, 7), (7, 6), (6, 5)),
-    2: ((0, 1), (0, 2), (2, 3), (2, 4), (0, 7), (0, 6), (6, 5)),
-    1: ((0, 1), (0, 2), (0, 3), (0, 4), (0, 7), (0, 6), (0, 5)),
-}
-Y_TREES = {2: ((0, 1), (1, 2), (0, 3)), 1: ((0, 1), (0, 2), (0, 3))}
-
 FLOWS = (
-    (0, 96, True, 3, 1, False),
-    (96, 160, False, 3, 1, True),
+    (0, 120, (0, 0, 3, 0, 0, 4, 10, 11, 4, 5, 11, 8, 8, 9, 15, 11, 24, 21, 26, 16, 16, 25, 21, 19, 0, 24, 27, 24, 31, 1, 29, 30)),
+    (120, 160, (0, 0, 1, 0, 0, 4, 5, 4, 4, 5, 6, 7, 0, 12, 13, 12, 24, 16, 19, 16, 24, 29, 21, 20, 0, 24, 27, 31, 0, 28, 2, 3)),
 )
 
 
 def tree_of(flow):
-    _, _, along_z, zt, yt, _ = flow
     children = {(rz, ry): [] for rz in range(NZ) for ry in range(NY)}
-    for a, b in Z_TREES[zt]:
-        for ry in range(1 if along_z else NY):
-            children[(a, ry)].append((b, ry))
-    for a, b in Y_TREES[yt]:
-        for rz in range(NZ if along_z else 1):
-            children[(rz, a)].append((rz, b))
+    for slot, parent in enumerate(flow[2]):
+        if slot:
+            children[divmod(parent, NY)].append(divmod(slot, NY))
     return children
 
 
@@ -61,7 +51,7 @@
     def height(f, node):
         return 1 + max((height(f, c) for c in TREES[f][node]), default=0)
 
-    heap = [(PICKS if FLOWS[f][5] else 0.0, f, (0, 0)) for f in range(len(FLOWS))]
+    heap = [(PICKS if (FLOWS[f][1] > PICKED) else 0.0, f, (0, 0)) for f in range(len(FLOWS))]
     free = {"z": 0.0, "y": 0.0}
     now, order = 0.0, []
     while heap:
@@ -87,8 +77,8 @@
 
 def gather_kernel(
     idx, cnt, grads, residual, momentum,
-    everyone, acc_out,
-    idx_s, cnt_s, idx_v, gbuf, rbuf,
+    everyone, acc_out, total,
+    idx_s, cnt_s, idx_v, gbuf, rbuf, keys, halves,
     send_sem, recv_sem, pair_send, pair_recv, in_sem, mom_sem, small_sem,
 ):
     me = lax.axis_index("dp")
@@ -117,7 +107,7 @@
     for b in range(2):
         small.append(
             pltpu.make_async_copy(
-                momentum.at[b, :, 0], everyone.at[0, 0, pl.ds(64 * b, 63)], mom_sem.at[b]
+                momentum.at[b, :, 0], everyone.at[0, 0, pl.ds(63 * b, 63)], mom_sem.at[b]
             )
         )
     for copy in small:
@@ -134,14 +124,14 @@
             loads.append((g, r))
     for copy in small:
         copy.wait()
-    offset = PITCH * lax.broadcasted_iota(jnp.int32, (2, 16), 0)
-    lists = (idx_v[0] + offset).astype(jnp.float32)
-    for q in range(8):
-        everyone[0, 0, 63:64, 16 * q : 16 * q + 16] = lists[q % 2 : q % 2 + 1]
+    lists = idx_v[0].astype(jnp.float32)
     lane = lax.broadcasted_iota(jnp.int32, (1, 128), 1)
-    own = lax.div(lane, 32) == lax.rem(me, 4)
-    everyone[0, 0, 63:64, :] = jnp.where(own, everyone[0, 0, 63:64, :], jnp.float32(0.0))
-    everyone[0, 0, 127:128, :] = jnp.zeros((1, 128), jnp.float32)
+    own = lax.div(lane, 16) == lax.rem(z, 2) * NY + y
+    for b in range(2):
+        at_row = pl.ds(126 + b, 1)
+        for q in range(8):
+            everyone[0, 0, at_row, 16 * q : 16 * q + 16] = lists[b : b + 1]
+        everyone[0, 0, at_row, :] = jnp.where(own, everyone[0, 0, at_row, :], jnp.float32(0.0))
 
     def piece(f, node, side=0):
         first, last = FLOWS[f][:2]
@@ -177,7 +167,7 @@
         across(f, node).start()
 
     for f, node, kids in ORDER:
-        if node == (0, 0) and not FLOWS[f][5]:
+        if node == (0, 0) and not (FLOWS[f][1] > PICKED):
             pass_on(f, node, kids)
     for b in range(2):
         for k in range(CHUNKS):
@@ -194,14 +184,38 @@
                 i < cnt_s[0, b], row, jnp.float32(0.0)
             )
     for f, node, kids in ORDER:
-        if node == (0, 0) and FLOWS[f][5]:
+        if node == (0, 0) and (FLOWS[f][1] > PICKED):
             pass_on(f, node, kids)
-    parent = {(f, kid): node for f, node, kids in ORDER for kid in kids}
-    for f, node, kids in ORDER:
-        if node != (0, 0):
-            hop(f, parent[(f, node)], node).wait_recv()
-            pass_on(f, node, kids)
-    for f in range(len(FLOWS)):
+    def collect():
+        for side in range(2):
+            way = turn if side == 0 else -turn
+            for pair in range(NZ // 2):
+                group = side * (NZ // 2) + pair
+                sums = [None, None]
+                for p in range(8):
+                    rz = 2 * pair + lax.rem(z + p // NY, 2)
+                    ry = lax.rem(way * (y - p % NY) + NY, NY)
+                    slot = rz * NY + ry
+                    for b in range(2):
+                        row = everyone[side, slot, pl.ds(126 + b, 1), :]
+                        sums[b] = row if sums[b] is None else sums[b] + row
+                        block = everyone[side, slot, pl.ds(PICKED + 16 * b, 16), :]
+                        high = block.astype(jnp.bfloat16)
+                        low = (block - high.astype(jnp.float32)).astype(jnp.bfloat16)
+                        k = pl.ds(128 * group + 16 * p, 16)
+                        halves[b, k, 0:128] = high
+                        halves[b, k, 128:256] = low
+                for b in range(2):
+                    keys[b, :, pl.ds(128 * group, 128)] = sums[b].astype(jnp.int32)
+
+    def sum_tile(t):
+        b, first = divmod(t * TILE, nb)
+        row = lax.broadcasted_iota(jnp.int32, (TILE, 1024), 0) + first
+        hit = (row == keys[b]).astype(jnp.float32).astype(jnp.bfloat16)
+        both = jnp.dot(hit, halves[b], preferred_element_type=jnp.float32)
+        total[b, pl.ds(first, TILE), :] = both[:, 0:128] + both[:, 128:256]
+
+    def settle(f):
         first, last = FLOWS[f][:2]
         span = pl.ds(first, last - first)
         others = everyone.at[0, pl.ds(1, SLOTS - 1), span]
@@ -210,19 +224,34 @@
         pair.wait_send()
         pair.wait_recv()
 
+    parent = {(f, kid): node for f, node, kids in ORDER for kid in kids}
+    later = [entry for entry in ORDER if entry[1] != (0, 0)]
+    collected = max(n for n, entry in enumerate(later) if entry[0] == len(FLOWS) - 1)
+    for n, (f, node, kids) in enumerate(later):
+        hop(f, parent[(f, node)], node).wait_recv()
+        pass_on(f, node, kids)
+        if n == collected:
+            settle(len(FLOWS) - 1)
+            collect()
+    for t in range(2 * nb // TILE):
+        sum_tile(t)
+    for f in range(len(FLOWS) - 1):
+        settle(f)
+
 
 def update_kernel(
-    sizes, idx_own, cnt, everyone, acc, params,
+    sizes, idx_own, cnt, everyone, acc, total, params,
     new_residual, new_momentum, new_params,
-    pbuf, nm, mine_v, lists_v, lists_s, zero_row, mom_sem, res_sem, row_sem, out_sem, list_sem,
+    pbuf, nm, mine_v, zero_row, mom_sem, res_sem, row_sem, out_sem,
 ):
     me = lax.axis_index("dp")
     core = lax.rem(me, 2)
     y = lax.rem(lax.div(me, 2), NY)
     z = lax.div(me, 2 * NY)
     nb = params.shape[1]
-    move = pltpu.make_async_copy(acc, new_residual.at[0], res_sem)
-    move.start()
+    moves = [pltpu.make_async_copy(acc.at[b], new_residual.at[0, b], res_sem.at[b]) for b in range(2)]
+    for move in moves:
+        move.start()
     zero_row[...] = jnp.zeros_like(zero_row)
 
     def place_of(o):
@@ -231,60 +260,30 @@
         slot = ((turn * (z - oz)) & (NZ - 1)) * NY + ((turn * (y - oy)) & (NY - 1))
         return (oc + core) & 1, slot
 
-    for q in range(16):
-        row = None
-        for o in range(4 * q, 4 * q + 4):
+    part = nb // CHUNKS
+    rows = new_momentum.shape[1]
+    outs = []
+    for b in range(2):
+
+        def place(o, carry):
+            start, mine = carry
             side, slot = place_of(o)
-            one = everyone[side, slot, 63:64, :]
-            row = one if row is None else row + one
-        lists_v[q : q + 1, :] = row.astype(jnp.int32)
-    fetch = pltpu.make_async_copy(lists_v, lists_s, list_sem)
-    fetch.start()
-
-    def place(o, carry):
-        s0, s1, m0, m1 = carry
-        side, slot = place_of(o)
-        nm[pl.ds(s0, 64), :] = decay_rate * everyone[side, slot, 0:64, :]
-        nm[pl.ds(s1, 64), :] = decay_rate * everyone[side, slot, 64:128, :]
-        m0 = jnp.where(o == me, s0, m0)
-        m1 = jnp.where(o == me, s1, m1)
-        return s0 + sizes[0, o], s1 + sizes[1, o], m0, m1
-
-    zero = jnp.int32(0)
-    _, _, m0, m1 = lax.fori_loop(0, 64, place, (zero, zero + PITCH, zero, zero), unroll=4)
-    fetch.wait()
-
-    def add(q, carry):
-        for k in range(4):
-            side, slot = place_of(4 * q + k)
-            for first in (0, 16):
-                rows = []
-                for i in range(first, first + 16):
-                    j = lists_s[q, 32 * k + i]
-                    rows.append((j, nm[pl.ds(j, 1), :] + everyone[side, slot, pl.ds(128 + i, 1), :]))
-                for j, row in rows:
-                    nm[pl.ds(j, 1), :] = row
-        return carry
-
-    lax.fori_loop(0, 16, add, 0)
-    part = nb // CHUNKS
-    outs = []
-    for b in range(2):
+            nm[b, pl.ds(start, 64), :] = decay_rate * everyone[side, slot, 63 * b : 63 * b + 64, :]
+            return start + sizes[b, o], jnp.where(o == me, start, mine)
+
+        _, first = lax.fori_loop(0, 64, place, (jnp.int32(0), jnp.int32(0)), unroll=8)
         for k in range(CHUNKS):
             span = pl.ds(k * part, part)
-            pbuf[b, span, :] = params[b, span, :] - learn_rate * nm[pl.ds(b * PITCH + k * part, part), :]
+            pbuf[b, span, :] = params[b, span, :] - learn_rate * (nm[b, span, :] + total[b, span, :])
             out = pltpu.make_async_copy(pbuf.at[b, span], new_params.at[b, span], out_sem.at[b * CHUNKS + k])
             out.start()
             outs.append(out)
-    rows = new_momentum.shape[1]
-    for b, first in ((0, m0), (1, m1)):
-        mine = nm[pl.ds(first, rows), :]
+        window = pl.ds(first, rows)
         inside = lax.broadcasted_iota(jnp.int32, (rows, 128), 0) < sizes[b, me]
-        mine_v[b] = jnp.where(inside, mine, jnp.float32(0.0))
+        mine_v[b] = jnp.where(inside, nm[b, window, :] + total[b, window, :], jnp.float32(0.0))
         out = pltpu.make_async_copy(mine_v.at[b], new_momentum.at[b, :, 0], mom_sem.at[b])
         out.start()
         outs.append(out)
-    move.wait()
 
     def clear(b, i):
         return pltpu.make_async_copy(
@@ -292,6 +291,7 @@
         )
 
     for b in range(2):
+        moves[b].wait()
         for i in range(16):
 
             @pl.when(i < cnt[0, b])
@@ -316,20 +316,23 @@
     vmem = pl.BlockSpec(memory_space=pltpu.VMEM)
     smem = pl.BlockSpec(memory_space=pltpu.SMEM)
     dma = pltpu.SemaphoreType.DMA
-    everyone, acc = pl.pallas_call(
+    everyone, acc, total = pl.pallas_call(
         gather_kernel,
         out_shape=(
             jax.ShapeDtypeStruct((2, SLOTS, ROWS, 128), jnp.float32),
             jax.ShapeDtypeStruct((2, nb, 128), jnp.float32),
+            jax.ShapeDtypeStruct((2, PITCH, 128), jnp.float32),
         ),
         in_specs=[hbm] * 5,
-        out_specs=(vmem, vmem),
+        out_specs=(vmem, vmem, vmem),
         scratch_shapes=[
             pltpu.SMEM(indices.shape, jnp.int32),
             pltpu.SMEM(counts.shape, jnp.int32),
             pltpu.VMEM(indices.shape, jnp.int32),
             pltpu.VMEM((2, nb, 128), jnp.bfloat16),
             pltpu.VMEM((2, nb, 128), jnp.float32),
+            pltpu.VMEM((2, 1, 1024), jnp.int32),
+            pltpu.VMEM((2, 1024, 256), jnp.bfloat16),
             dma((len(FLOWS),)),
             dma((len(FLOWS), SLOTS)),
             dma((len(FLOWS),)),
@@ -351,24 +354,21 @@
             jax.ShapeDtypeStruct((2, rows, 1, 128), jnp.float32),
             jax.ShapeDtypeStruct(params.shape, jnp.float32),
         ),
-        in_specs=[smem, smem, smem, vmem, vmem, vmem],
+        in_specs=[smem, smem, smem, vmem, vmem, vmem, vmem],
         out_specs=(any_space, any_space, any_space),
         scratch_shapes=[
             pltpu.VMEM((2, nb, 128), jnp.float32),
-            pltpu.VMEM((2 * PITCH, 128), jnp.float32),
+            pltpu.VMEM((2, PITCH, 128), jnp.float32),
             pltpu.VMEM((2, rows, 128), jnp.float32),
-            pltpu.VMEM((16, 128), jnp.int32),
-            pltpu.SMEM((16, 128), jnp.int32),
             pltpu.VMEM((1, 128), jnp.float32),
             dma((2,)),
-            dma,
+            dma((2,)),
             dma((2, 16)),
             dma((2 * CHUNKS,)),
-            dma,
         ],
         compiler_params=pltpu.CompilerParams(vmem_limit_bytes=32 << 20),
         name="update",
-    )(region_sizes, indices, counts, everyone, acc, params)
+    )(region_sizes, indices, counts, everyone, acc, total, params)
     return new_residual, jnp.swapaxes(new_momentum, 1, 2), new_params
 
 

time: 39 us -> 37.7 us (0.967)
  Pallas kernels: 38.2 us -> 36.9 us
    pallas_call x1, Pallas kernels: 5.99 us -> 3.41 us  [on_device(): pl.pallas_call(update_kernel, out_shape=(jax.ShapeDtypeStruct((1, 2, nb,...]
    pallas_call x1, Pallas kernels: 32.2 us -> 33.5 us  [on_device(): pl.pallas_call(gather_kernel, out_shape=(jax.ShapeDtypeStruct((2, SLOTS,...]
where the time goes in v3:
time: 37.7 us; the launch traced here: 37.6 us
  Pallas kernels  36.9 us (98%)
  between operations  0.7 us (2%)
    pallas_call x1, Pallas kernels, on_device(): pl.pallas_call(gather_kernel, out_shape=(jax.ShapeDtypeStruct((2, SLOTS,...  33.5 us
    pallas_call x1, Pallas kernels, on_device(): pl.pallas_call(update_kernel, out_shape=(jax.ShapeDtypeStruct((1, 2, nb,...  3.41 us

profile of v3, /device:TPU:1, one launch (start us, length us, event | category | flops | bytes accessed | tf_op | source)
XLA Modules:
  0.0 37.6 jit_solution(7087873897613127227)
XLA Ops:
  0.6 0.0 copy-start.2
  0.6 0.0 copy-start.1
  0.7 0.0 copy-start.3
  0.7 0.0 copy-start
  0.7 33.5 %gather.1 = (f32[2,32,160,128]{3,2,1,0:T(8,128)S(1)}, f32[2,2048,128]{2,1,0:T(8,128)S(1)}, f32[2,2112,128]{2,1,0:T(8,128)S(1)}) custom-call(s32[1,2,16]{2,1,0:T(2,128)} %idx_own.1, s32[1,2]{1,0:T(1,128)} %cnt.3, bf16[1,2,2048,128]{3,2,1,0:T(8,128)(2,1)} %grads.1, f32[1,2,2048,128]{3,2,1,0:T(8,128)} %residual.1, f32[2,63,1,128]{3,2,1,0:T(1,128)} %bitcast.2), custom_call_target="tpu_custom_call" | custom-call | tf_op jit(solution)/shard_map/gather/pallas_call | solution.py:319
  34.2 0.0 copy-done.2
  34.2 0.0 copy-done.1
  34.2 0.0 copy-done.3
  34.2 0.0 copy-done
  34.2 3.4 %update.1 = (f32[1,2,2048,128]{3,2,1,0:T(8,128)}, f32[2,63,1,128]{3,2,1,0:T(1,128)}, f32[2,2048,128]{2,1,0:T(8,128)}) custom-call(s32[2,64]{1,0:T(2,128)S(1)} %copy-done.3, s32[1,2,16]{2,1,0:T(2,128)S(1)} %copy-done.1, s32[1,2]{1,0:T(1,128)S(1)} %copy-done.2, f32[2,32,160,128]{3,2,1,0:T(8,128)S(1)} %get-tuple-element.9.everyone, ...), custom_call_target="tpu_custom_call" | custom-call | tf_op jit(solution)/shard_map/update/pallas_call | solution.py:350
Async XLA Ops:
  0.6 33.6 %copy-start.2 = (s32[1,2]{1,0:T(1,128)S(1)}, s32[1,2]{1,0:T(1,128)}, u32[]{:S(2)}) copy-start(s32[1,2]{1,0:T(1,128)} %cnt.3) | copy-start | bytes 28
  0.6 33.6 %copy-start.1 = (s32[1,2,16]{2,1,0:T(2,128)S(1)}, s32[1,2,16]{2,1,0:T(2,128)}, u32[]{:S(2)}) copy-start(s32[1,2,16]{2,1,0:T(2,128)} %idx_own.1) | copy-start | bytes 388
  0.7 33.6 %copy-start.3 = (s32[2,64]{1,0:T(2,128)S(1)}, s32[2,64]{1,0:T(2,128)}, u32[]{:S(2)}) copy-start(s32[2,64]{1,0:T(2,128)} %sizes.1) | copy-start | bytes 1540
  0.7 33.6 %copy-start = (f32[2,2048,128]{2,1,0:T(8,128)S(1)}, f32[2,2048,128]{2,1,0:T(8,128)}, u32[]{:S(2)}) copy-start(f32[2,2048,128]{2,1,0:T(8,128)} %params.1) | copy-start | bytes 6291460

commit v4 on v3

--- a/solution.py
+++ b/solution.py
@@ -22,8 +22,8 @@
 
 
 FLOWS = (
-    (0, 120, (0, 0, 3, 0, 0, 4, 10, 11, 4, 5, 11, 8, 8, 9, 15, 11, 24, 21, 26, 16, 16, 25, 21, 19, 0, 24, 27, 24, 31, 1, 29, 30)),
-    (120, 160, (0, 0, 1, 0, 0, 4, 5, 4, 4, 5, 6, 7, 0, 12, 13, 12, 24, 16, 19, 16, 24, 29, 21, 20, 0, 24, 27, 31, 0, 28, 2, 3)),
+    (0, 80, (0, 0, 22, 0, 0, 4, 5, 3, 4, 13, 6, 7, 8, 12, 15, 12, 12, 16, 22, 16, 23, 20, 23, 3, 20, 24, 22, 31, 0, 28, 31, 28)),
+    (80, 160, (0, 0, 0, 2, 5, 6, 2, 6, 0, 8, 8, 10, 8, 12, 10, 12, 24, 16, 26, 18, 12, 20, 26, 20, 0, 24, 2, 31, 0, 28, 31, 28)),
 )
 
 
@@ -186,34 +186,37 @@
     for f, node, kids in ORDER:
         if node == (0, 0) and (FLOWS[f][1] > PICKED):
             pass_on(f, node, kids)
-    def collect():
-        for side in range(2):
-            way = turn if side == 0 else -turn
-            for pair in range(NZ // 2):
-                group = side * (NZ // 2) + pair
-                sums = [None, None]
-                for p in range(8):
-                    rz = 2 * pair + lax.rem(z + p // NY, 2)
-                    ry = lax.rem(way * (y - p % NY) + NY, NY)
-                    slot = rz * NY + ry
-                    for b in range(2):
-                        row = everyone[side, slot, pl.ds(126 + b, 1), :]
-                        sums[b] = row if sums[b] is None else sums[b] + row
-                        block = everyone[side, slot, pl.ds(PICKED + 16 * b, 16), :]
-                        high = block.astype(jnp.bfloat16)
-                        low = (block - high.astype(jnp.float32)).astype(jnp.bfloat16)
-                        k = pl.ds(128 * group + 16 * p, 16)
-                        halves[b, k, 0:128] = high
-                        halves[b, k, 128:256] = low
+    def collect(side):
+        way = turn if side == 0 else -turn
+        for pair in range(NZ // 2):
+            group = side * (NZ // 2) + pair
+            sums = [None, None]
+            for p in range(8):
+                rz = 2 * pair + lax.rem(z + p // NY, 2)
+                ry = lax.rem(way * (y - p % NY) + NY, NY)
+                slot = rz * NY + ry
                 for b in range(2):
-                    keys[b, :, pl.ds(128 * group, 128)] = sums[b].astype(jnp.int32)
-
-    def sum_tile(t):
+                    row = everyone[side, slot, pl.ds(126 + b, 1), :]
+                    sums[b] = row if sums[b] is None else sums[b] + row
+                    block = everyone[side, slot, pl.ds(PICKED + 16 * b, 16), :]
+                    high = block.astype(jnp.bfloat16)
+                    low = (block - high.astype(jnp.float32)).astype(jnp.bfloat16)
+                    k = pl.ds(128 * group + 16 * p, 16)
+                    halves[b, k, 0:128] = high
+                    halves[b, k, 128:256] = low
+            for b in range(2):
+                keys[b, :, pl.ds(128 * group, 128)] = sums[b].astype(jnp.int32)
+
+    def sum_tile(t, side):
         b, first = divmod(t * TILE, nb)
-        row = lax.broadcasted_iota(jnp.int32, (TILE, 1024), 0) + first
-        hit = (row == keys[b]).astype(jnp.float32).astype(jnp.bfloat16)
-        both = jnp.dot(hit, halves[b], preferred_element_type=jnp.float32)
-        total[b, pl.ds(first, TILE), :] = both[:, 0:128] + both[:, 128:256]
+        k = pl.ds(512 * side, 512)
+        row = lax.broadcasted_iota(jnp.int32, (TILE, 512), 0) + first
+        hit = (row == keys[b, :, k]).astype(jnp.float32).astype(jnp.bfloat16)
+        both = jnp.dot(hit, halves[b, k, :], preferred_element_type=jnp.float32)
+        tile = both[:, 0:128] + both[:, 128:256]
+        if side:
+            tile = tile + total[b, pl.ds(first, TILE), :]
+        total[b, pl.ds(first, TILE), :] = tile
 
     def settle(f):
         first, last = FLOWS[f][:2]
@@ -226,15 +229,15 @@
 
     parent = {(f, kid): node for f, node, kids in ORDER for kid in kids}
     later = [entry for entry in ORDER if entry[1] != (0, 0)]
-    collected = max(n for n, entry in enumerate(later) if entry[0] == len(FLOWS) - 1)
-    for n, (f, node, kids) in enumerate(later):
+    for f, node, kids in later:
         hop(f, parent[(f, node)], node).wait_recv()
         pass_on(f, node, kids)
-        if n == collected:
+    for side in range(2):
+        if side:
             settle(len(FLOWS) - 1)
-            collect()
-    for t in range(2 * nb // TILE):
-        sum_tile(t)
+        collect(side)
+        for t in range(2 * nb // TILE):
+            sum_tile(t, side)
     for f in range(len(FLOWS) - 1):
         settle(f)
 

time: 37.7 us -> 36.8 us (0.976)
  Pallas kernels: 36.9 us -> 35.8 us
    pallas_call x1, Pallas kernels: 33.5 us -> 32.4 us  [on_device(): pl.pallas_call(gather_kernel, out_shape=(jax.ShapeDtypeStruct((2, SLOTS,...]
where the time goes in v4:
time: 36.8 us; the launch traced here: 36.5 us
  Pallas kernels  35.8 us (97%)
  between operations  0.7 us (2%)
    pallas_call x1, Pallas kernels, on_device(): pl.pallas_call(gather_kernel, out_shape=(jax.ShapeDtypeStruct((2, SLOTS,...  32.4 us
    pallas_call x1, Pallas kernels, on_device(): pl.pallas_call(update_kernel, out_shape=(jax.ShapeDtypeStruct((1, 2, nb,...  3.39 us

profile of v4, /device:TPU:1, one launch (start us, length us, event | category | flops | bytes accessed | tf_op | source)
XLA Modules:
  0.0 36.5 jit_solution(11792630954190951345)
XLA Ops:
  0.6 0.0 copy-start.2
  0.6 0.0 copy-start.1
  0.7 0.0 copy-start.3
  0.7 0.0 copy-start
  0.7 32.4 %gather.1 = (f32[2,32,160,128]{3,2,1,0:T(8,128)S(1)}, f32[2,2048,128]{2,1,0:T(8,128)S(1)}, f32[2,2112,128]{2,1,0:T(8,128)S(1)}) custom-call(s32[1,2,16]{2,1,0:T(2,128)} %idx_own.1, s32[1,2]{1,0:T(1,128)} %cnt.3, bf16[1,2,2048,128]{3,2,1,0:T(8,128)(2,1)} %grads.1, f32[1,2,2048,128]{3,2,1,0:T(8,128)} %residual.1, f32[2,63,1,128]{3,2,1,0:T(1,128)} %bitcast.2), custom_call_target="tpu_custom_call" | custom-call | tf_op jit(solution)/shard_map/gather/pallas_call | solution.py:322
  33.1 0.0 copy-done.2
  33.1 0.0 copy-done.1
  33.1 0.0 copy-done.3
  33.1 0.0 copy-done
  33.1 3.4 %update.1 = (f32[1,2,2048,128]{3,2,1,0:T(8,128)}, f32[2,63,1,128]{3,2,1,0:T(1,128)}, f32[2,2048,128]{2,1,0:T(8,128)}) custom-call(s32[2,64]{1,0:T(2,128)S(1)} %copy-done.3, s32[1,2,16]{2,1,0:T(2,128)S(1)} %copy-done.1, s32[1,2]{1,0:T(1,128)S(1)} %copy-done.2, f32[2,32,160,128]{3,2,1,0:T(8,128)S(1)} %get-tuple-element.9.everyone, ...), custom_call_target="tpu_custom_call" | custom-call | tf_op jit(solution)/shard_map/update/pallas_call | solution.py:353
Async XLA Ops:
  0.6 32.4 %copy-start.2 = (s32[1,2]{1,0:T(1,128)S(1)}, s32[1,2]{1,0:T(1,128)}, u32[]{:S(2)}) copy-start(s32[1,2]{1,0:T(1,128)} %cnt.3) | copy-start | bytes 28
  0.6 32.4 %copy-start.1 = (s32[1,2,16]{2,1,0:T(2,128)S(1)}, s32[1,2,16]{2,1,0:T(2,128)}, u32[]{:S(2)}) copy-start(s32[1,2,16]{2,1,0:T(2,128)} %idx_own.1) | copy-start | bytes 388
  0.7 32.4 %copy-start.3 = (s32[2,64]{1,0:T(2,128)S(1)}, s32[2,64]{1,0:T(2,128)}, u32[]{:S(2)}) copy-start(s32[2,64]{1,0:T(2,128)} %sizes.1) | copy-start | bytes 1540
  0.7 32.4 %copy-start = (f32[2,2048,128]{2,1,0:T(8,128)S(1)}, f32[2,2048,128]{2,1,0:T(8,128)}, u32[]{:S(2)}) copy-start(f32[2,2048,128]{2,1,0:T(8,128)} %params.1) | copy-start | bytes 6291460

commit v5 on v4

--- a/solution.py
+++ b/solution.py
@@ -16,7 +16,7 @@
 ROWS = 160
 MESH = pl.DeviceIdType.MESH
 CHUNKS = 4
-TILE = 256
+TILE = 512
 PICKED = 128
 PITCH = 2048 + 64
 
@@ -44,7 +44,7 @@
 
 
 STEPS = tuple(sorted({step_of(n, k) for t in TREES for n, kids in t.items() for k in kids}))
-LATENCY, PER_HOP, PICKS = 1.6, 0.65, 1.5
+LATENCY, PER_HOP, PICKS = 2.0, 0.65, 1.5
 
 
 def schedule():
@@ -56,14 +56,14 @@
     now, order = 0.0, []
     while heap:
         at, f, node = heapq.heappop(heap)
-        now = max(now, at) + 0.05
+        now = max(now, at) + 0.02
         kids = sorted(TREES[f][node], key=lambda c: -height(f, c))
         order.append((f, node, kids))
         for kid in kids:
-            now += 0.07
+            now += 0.02
             dz, dy = step_of(node, kid)
             axis, hops = ("z", abs(dz)) if dz else ("y", abs(dy))
-            free[axis] = max(free[axis], now) + hops * (FLOWS[f][1] - FLOWS[f][0]) * 512 / 105e3
+            free[axis] = max(free[axis], now) + hops * (FLOWS[f][1] - FLOWS[f][0]) * 512 / 102e3
             heapq.heappush(heap, (free[axis] + LATENCY + hops * PER_HOP, f, kid))
     return order
 
@@ -186,10 +186,9 @@
     for f, node, kids in ORDER:
         if node == (0, 0) and (FLOWS[f][1] > PICKED):
             pass_on(f, node, kids)
-    def collect(side):
+    def collect(side, pairs, group):
         way = turn if side == 0 else -turn
-        for pair in range(NZ // 2):
-            group = side * (NZ // 2) + pair
+        for group, pair in enumerate(pairs, group):
             sums = [None, None]
             for p in range(8):
                 rz = 2 * pair + lax.rem(z + p // NY, 2)
@@ -207,14 +206,14 @@
             for b in range(2):
                 keys[b, :, pl.ds(128 * group, 128)] = sums[b].astype(jnp.int32)
 
-    def sum_tile(t, side):
+    def sum_tile(t, first_k, keys_n):
         b, first = divmod(t * TILE, nb)
-        k = pl.ds(512 * side, 512)
-        row = lax.broadcasted_iota(jnp.int32, (TILE, 512), 0) + first
+        k = pl.ds(first_k, keys_n)
+        row = lax.broadcasted_iota(jnp.int32, (TILE, keys_n), 0) + first
         hit = (row == keys[b, :, k]).astype(jnp.float32).astype(jnp.bfloat16)
         both = jnp.dot(hit, halves[b, k, :], preferred_element_type=jnp.float32)
         tile = both[:, 0:128] + both[:, 128:256]
-        if side:
+        if first_k:
             tile = tile + total[b, pl.ds(first, TILE), :]
         total[b, pl.ds(first, TILE), :] = tile
 
@@ -229,15 +228,25 @@
 
     parent = {(f, kid): node for f, node, kids in ORDER for kid in kids}
     later = [entry for entry in ORDER if entry[1] != (0, 0)]
-    for f, node, kids in later:
+    def add_blocks(side, pairs, group):
+        collect(side, pairs, group)
+        for t in range(2 * nb // TILE):
+            sum_tile(t, 128 * group, 128 * len(pairs))
+
+    sent = max(n for n, entry in enumerate(later) if entry[2])
+    here = {entry[1][0] for entry in later[sent + 1 :] if entry[0] == len(FLOWS) - 1}
+    pairs = range(NZ // 2)
+    whole = [p for p in pairs if not here & {2 * p, 2 * p + 1}]
+    for n, (f, node, kids) in enumerate(later):
         hop(f, parent[(f, node)], node).wait_recv()
         pass_on(f, node, kids)
-    for side in range(2):
-        if side:
-            settle(len(FLOWS) - 1)
-        collect(side)
-        for t in range(2 * nb // TILE):
-            sum_tile(t, side)
+        if n == sent and whole:
+            add_blocks(0, whole, 0)
+    rest = [p for p in pairs if p not in whole]
+    if rest:
+        add_blocks(0, rest, len(whole))
+    settle(len(FLOWS) - 1)
+    add_blocks(1, pairs, len(pairs))
     for f in range(len(FLOWS) - 1):
         settle(f)
 

time: 36.8 us -> 36.1 us (0.981)
  Pallas kernels: 35.8 us -> 35.3 us
    pallas_call x1, Pallas kernels: 32.4 us -> 31.9 us  [on_device(): pl.pallas_call(gather_kernel, out_shape=(jax.ShapeDtypeStruct((2, SLOTS,...]
where the time goes in v5:
time: 36.1 us; the launch traced here: 36 us
  Pallas kernels  35.3 us (98%)
  between operations  0.7 us (2%)
    pallas_call x1, Pallas kernels, on_device(): pl.pallas_call(gather_kernel, out_shape=(jax.ShapeDtypeStruct((2, SLOTS,...  31.9 us
    pallas_call x1, Pallas kernels, on_device(): pl.pallas_call(update_kernel, out_shape=(jax.ShapeDtypeStruct((1, 2, nb,...  3.39 us

profile of v5, /device:TPU:1, one launch (start us, length us, event | category | flops | bytes accessed | tf_op | source)
XLA Modules:
  0.0 36.0 jit_solution(5440354759864413712)
XLA Ops:
  0.6 0.0 copy-start.2
  0.6 0.0 copy-start.1
  0.7 0.0 copy-start.3
  0.7 0.0 copy-start
  0.7 31.9 %gather.1 = (f32[2,32,160,128]{3,2,1,0:T(8,128)S(1)}, f32[2,2048,128]{2,1,0:T(8,128)S(1)}, f32[2,2112,128]{2,1,0:T(8,128)S(1)}) custom-call(s32[1,2,16]{2,1,0:T(2,128)} %idx_own.1, s32[1,2]{1,0:T(1,128)} %cnt.3, bf16[1,2,2048,128]{3,2,1,0:T(8,128)(2,1)} %grads.1, f32[1,2,2048,128]{3,2,1,0:T(8,128)} %residual.1, f32[2,63,1,128]{3,2,1,0:T(1,128)} %bitcast.2), custom_call_target="tpu_custom_call" | custom-call | tf_op jit(solution)/shard_map/gather/pallas_call | solution.py:331
  32.6 0.0 copy-done.2
  32.6 0.0 copy-done.1
  32.6 0.0 copy-done.3
  32.6 0.0 copy-done
  32.6 3.4 %update.1 = (f32[1,2,2048,128]{3,2,1,0:T(8,128)}, f32[2,63,1,128]{3,2,1,0:T(1,128)}, f32[2,2048,128]{2,1,0:T(8,128)}) custom-call(s32[2,64]{1,0:T(2,128)S(1)} %copy-done.3, s32[1,2,16]{2,1,0:T(2,128)S(1)} %copy-done.1, s32[1,2]{1,0:T(1,128)S(1)} %copy-done.2, f32[2,32,160,128]{3,2,1,0:T(8,128)S(1)} %get-tuple-element.9.everyone, ...), custom_call_target="tpu_custom_call" | custom-call | tf_op jit(solution)/shard_map/update/pallas_call | solution.py:362
Async XLA Ops:
  0.6 32.0 %copy-start.2 = (s32[1,2]{1,0:T(1,128)S(1)}, s32[1,2]{1,0:T(1,128)}, u32[]{:S(2)}) copy-start(s32[1,2]{1,0:T(1,128)} %cnt.3) | copy-start | bytes 28
  0.6 32.0 %copy-start.1 = (s32[1,2,16]{2,1,0:T(2,128)S(1)}, s32[1,2,16]{2,1,0:T(2,128)}, u32[]{:S(2)}) copy-start(s32[1,2,16]{2,1,0:T(2,128)} %idx_own.1) | copy-start | bytes 388
  0.7 32.0 %copy-start.3 = (s32[2,64]{1,0:T(2,128)S(1)}, s32[2,64]{1,0:T(2,128)}, u32[]{:S(2)}) copy-start(s32[2,64]{1,0:T(2,128)} %sizes.1) | copy-start | bytes 1540
  0.7 32.0 %copy-start = (f32[2,2048,128]{2,1,0:T(8,128)S(1)}, f32[2,2048,128]{2,1,0:T(8,128)}, u32[]{:S(2)}) copy-start(f32[2,2048,128]{2,1,0:T(8,128)} %params.1) | copy-start | bytes 6291460

commit v6 on v5

--- a/solution.py
+++ b/solution.py
@@ -157,7 +157,8 @@
         )
 
     def across(f, node):
-        return remote(piece(f, node), piece(f, node, 1), pair_send.at[f], pair_recv.at[f], sibling)
+        arrived = f + node[0] // 2 if f == len(FLOWS) - 1 else f
+        return remote(piece(f, node), piece(f, node, 1), pair_send.at[f], pair_recv.at[arrived], sibling)
 
     pl.semaphore_wait(barrier, len(STEPS) + 1)
 
@@ -224,14 +225,31 @@
         remote(others, others, send_sem.at[f], pair_recv.at[f], sibling).wait_send()
         pair = remote(everyone.at[0, :, span], everyone.at[1, :, span], pair_send.at[f], pair_recv.at[f], sibling)
         pair.wait_send()
-        pair.wait_recv()
+        if f < len(FLOWS) - 1:
+            pair.wait_recv()
 
     parent = {(f, kid): node for f, node, kids in ORDER for kid in kids}
     later = [entry for entry in ORDER if entry[1] != (0, 0)]
-    def add_blocks(side, pairs, group):
-        collect(side, pairs, group)
+    def add_blocks(group, *parts):
+        count = 0
+        for side, some in parts:
+            collect(side, some, group + count)
+            count += len(some)
         for t in range(2 * nb // TILE):
-            sum_tile(t, 128 * group, 128 * len(pairs))
+            sum_tile(t, 128 * group, 128 * count)
+
+    def arrive(some):
+        first, last = FLOWS[-1][:2]
+        span = pl.ds(first, last - first)
+        for p in some:
+            slots = pl.ds(2 * NY * p, 2 * NY)
+            remote(
+                everyone.at[0, slots, span],
+                everyone.at[1, slots, span],
+                pair_send.at[len(FLOWS) - 1],
+                pair_recv.at[len(FLOWS) - 1 + p],
+                sibling,
+            ).wait_recv()
 
     sent = max(n for n, entry in enumerate(later) if entry[2])
     here = {entry[1][0] for entry in later[sent + 1 :] if entry[0] == len(FLOWS) - 1}
@@ -241,13 +259,14 @@
         hop(f, parent[(f, node)], node).wait_recv()
         pass_on(f, node, kids)
         if n == sent and whole:
-            add_blocks(0, whole, 0)
+            arrive(whole)
+            add_blocks(0, (0, whole), (1, whole))
     rest = [p for p in pairs if p not in whole]
     if rest:
-        add_blocks(0, rest, len(whole))
-    settle(len(FLOWS) - 1)
-    add_blocks(1, pairs, len(pairs))
-    for f in range(len(FLOWS) - 1):
+        add_blocks(2 * len(whole), (0, rest))
+        arrive(rest)
+        add_blocks(2 * len(whole) + len(rest), (1, rest))
+    for f in range(len(FLOWS)):
         settle(f)
 
 
@@ -348,7 +367,7 @@
             dma((len(FLOWS),)),
             dma((len(FLOWS), SLOTS)),
             dma((len(FLOWS),)),
-            dma((len(FLOWS),)),
+            dma((len(FLOWS) + NZ // 2 - 1,)),
             dma((2, 2 * CHUNKS)),
             dma((2,)),
             dma((3,)),

time: 36.1 us -> 36.1 us (level)
  no operation moved by 1% of the time
where the time goes in v6:
time: 36.1 us; the launch traced here: 36 us
  Pallas kernels  35.3 us (98%)
  between operations  0.7 us (2%)
    pallas_call x1, Pallas kernels, on_device(): pl.pallas_call(gather_kernel, out_shape=(jax.ShapeDtypeStruct((2, SLOTS,...  31.9 us
    pallas_call x1, Pallas kernels, on_device(): pl.pallas_call(update_kernel, out_shape=(jax.ShapeDtypeStruct((1, 2, nb,...  3.41 us

profile of v6, /device:TPU:1, one launch (start us, length us, event | category | flops | bytes accessed | tf_op | source)
XLA Modules:
  0.0 36.0 jit_solution(15327407823328876160)
XLA Ops:
  0.6 0.0 copy-start.2
  0.6 0.0 copy-start.1
  0.7 0.0 copy-start.3
  0.7 0.0 copy-start
  0.7 31.9 %gather.1 = (f32[2,32,160,128]{3,2,1,0:T(8,128)S(1)}, f32[2,2048,128]{2,1,0:T(8,128)S(1)}, f32[2,2112,128]{2,1,0:T(8,128)S(1)}) custom-call(s32[1,2,16]{2,1,0:T(2,128)} %idx_own.1, s32[1,2]{1,0:T(1,128)} %cnt.3, bf16[1,2,2048,128]{3,2,1,0:T(8,128)(2,1)} %grads.1, f32[1,2,2048,128]{3,2,1,0:T(8,128)} %residual.1, f32[2,63,1,128]{3,2,1,0:T(1,128)} %bitcast.2), custom_call_target="tpu_custom_call" | custom-call | tf_op jit(solution)/shard_map/gather/pallas_call | solution.py:350
  32.6 0.0 copy-done.2
  32.6 0.0 copy-done.1
  32.6 0.0 copy-done.3
  32.6 0.0 copy-done
  32.6 3.4 %update.1 = (f32[1,2,2048,128]{3,2,1,0:T(8,128)}, f32[2,63,1,128]{3,2,1,0:T(1,128)}, f32[2,2048,128]{2,1,0:T(8,128)}) custom-call(s32[2,64]{1,0:T(2,128)S(1)} %copy-done.3, s32[1,2,16]{2,1,0:T(2,128)S(1)} %copy-done.1, s32[1,2]{1,0:T(1,128)S(1)} %copy-done.2, f32[2,32,160,128]{3,2,1,0:T(8,128)S(1)} %get-tuple-element.9.everyone, ...), custom_call_target="tpu_custom_call" | custom-call | tf_op jit(solution)/shard_map/update/pallas_call | solution.py:381
Async XLA Ops:
  0.6 31.9 %copy-start.2 = (s32[1,2]{1,0:T(1,128)S(1)}, s32[1,2]{1,0:T(1,128)}, u32[]{:S(2)}) copy-start(s32[1,2]{1,0:T(1,128)} %cnt.3) | copy-start | bytes 28
  0.6 31.9 %copy-start.1 = (s32[1,2,16]{2,1,0:T(2,128)S(1)}, s32[1,2,16]{2,1,0:T(2,128)}, u32[]{:S(2)}) copy-start(s32[1,2,16]{2,1,0:T(2,128)} %idx_own.1) | copy-start | bytes 388
  0.7 31.9 %copy-start.3 = (s32[2,64]{1,0:T(2,128)S(1)}, s32[2,64]{1,0:T(2,128)}, u32[]{:S(2)}) copy-start(s32[2,64]{1,0:T(2,128)} %sizes.1) | copy-start | bytes 1540
  0.7 31.9 %copy-start = (f32[2,2048,128]{2,1,0:T(8,128)S(1)}, f32[2,2048,128]{2,1,0:T(8,128)}, u32[]{:S(2)}) copy-start(f32[2,2048,128]{2,1,0:T(8,128)} %params.1) | copy-start | bytes 6291460
